TPU v7x, 512 devices: a whole 4x8x8 slice. The times are simulated.
512 devices in a mesh: pair: 32 (over z_hi, y, core), split: 16 (over x, z_lo).
Axes of the slice: x: 4, y: 8, z: 8 (z_hi: 2, z_lo: 4; z = z_hi * 4 + z_lo), core: 2. Of those that a mesh axis runs over, the one named last changes fastest.
Arguments:
- integrals: bfloat16 [8192, 10240], P('pair', 'split'), may hold values from -0.109375 to 0.109375
- normal_ops: bfloat16 [10240, 8192], P('split', 'pair'), may hold values from -6 to 6
- window: int32 [10240], P('split'), may hold values 0 or 1
Outputs:
- complementary: bfloat16 [8192, 8192], P(('pair', 'split'))
All inputs are finite; a program needn't handle non-finite values. No bound on the sum of `window` on one device may be relied on, other than what follows from the above.
Results may differ from a plain program's by a relative error of at most 0.001.
Values may be sent and summed in bfloat16 or wider, within the bound.
A program may use at most 64 MiB of HBM per device.

v0:
```python
import jax
import jax.numpy as jnp
from jax import lax
from jax.sharding import PartitionSpec as P


def on_device(integrals, normal_ops, window):
    windowed = normal_ops * window[:, None].astype(jnp.bfloat16)
    partial_term = jnp.dot(
        integrals,
        lax.all_gather(windowed, "pair", axis=1, tiled=True),
        preferred_element_type=jnp.float32,
    )
    result = lax.psum_scatter(partial_term, "split", scatter_dimension=0, tiled=True)
    return result.astype(jnp.bfloat16)


def solution(mesh):
    placed = (P("pair", "split"), P("split", "pair"), P("split"))
    return jax.shard_map(
        on_device, mesh=mesh, in_specs=placed, out_specs=P(("pair", "split"), None), check_vma=False
    )
```

profile of v0, /device:TPU:1, one launch (start us, length us, event | category | flops | bytes accessed | tf_op | source)
XLA Modules:
  0.0 388.2 jit_solution(11485793355978395272)
XLA Ops:
  6.5 0.0 copy-start
  6.5 0.0 all-gather.2.cloned.1.call-start
  6.5 0.7 convert_element_type.7
  7.3 1.9 broadcast_multiply_fusion
  9.1 0.0 all-gather.2.cloned.1.call-update
  9.2 0.0 reduce-scatter.4.cloned.1.call-start
  9.2 166.4 %all-gather.2.cloned.1.call-done = bf16[640,8192]{1,0:T(8,128)(2,1)} async-done(((bf16[640,256]{1,0:T(8,128)(2,1)}), bf16[640,8192]{1,0:T(8,128)(2,1)}) %all-gather.2.cloned.1.call-update) | async-done | bytes 10485776 | tf_op jit(solution)/shard_map/all_gather | solution.py:11
  175.6 0.0 copy-done
  175.6 10.8 %convolution_bitcast_fusion = f32[256,8192]{0,1:T(8,128)} fusion(bf16[640,8192]{1,0:T(8,128)(2,1)} %all-gather.2.cloned.1.call-done, bf16[256,640]{1,0:T(8,128)(2,1)S(1)} %copy-done), kind=kOutput, calls=%fused_computation | convolution fusion | flops 2684354560 | bytes 19202048 | tf_op jit(solution)/shard_map/dot_general | solution.py:9
  186.4 8.9 %copy.7 = f32[256,8192]{1,0:T(8,128)} copy(f32[256,8192]{0,1:T(8,128)} %convolution_bitcast_fusion) | data formatting | bytes 16777216
  195.3 0.0 reduce-scatter.4.cloned.1.call-update
  195.3 184.2 %reduce-scatter.4.cloned.1.call-done = f32[16,8192]{1,0:T(8,128)} async-done(((f32[256,8192]{1,0:T(8,128)}), f32[16,8192]{1,0:T(8,128)}) %reduce-scatter.4.cloned.1.call-update) | async-done | bytes 524304 | tf_op jit(solution)/shard_map/reduce_scatter | solution.py:14
  379.6 1.8 convert_element_type.8
Async XLA Ops:
  6.5 169.0 %copy-start = (bf16[256,640]{1,0:T(8,128)(2,1)S(1)}, bf16[256,640]{1,0:T(8,128)(2,1)}, u32[]{:S(2)}) copy-start(bf16[256,640]{1,0:T(8,128)(2,1)} %param.3) | copy-start | bytes 983044
  6.5 169.0 %all-gather.2.cloned.1.call-start = ((), (), s32[]{:S(2)}) async-start(), calls=%async_computation.1 | async-start | bytes 10813440 | tf_op jit(solution)/shard_map/all_gather | solution.py:11
  9.2 370.4 %reduce-scatter.4.cloned.1.call-start = ((), (), s32[]{:S(2)}) async-start(), calls=%async_computation.2 | async-start | bytes 8912896 | tf_op jit(solution)/shard_map/reduce_scatter | solution.py:14
Sparse Core Ops, SparseCore 0:
  10.5 165.0 all-gather.1
  195.4 184.0 reduce-scatter.3
where the time goes:
time: 389 us; the launch traced here: 388 us
  waiting for transfers between devices  351 us (90%)
  between operations  13.4 us (3%)
  matrix products  10.8 us (3%)
  local copies, waits for them, and re-layouts  8.94 us (2%)
  other arithmetic  4.36 us (1%)
    reduce_scatter x1, waiting for transfers between devices, on_device(): lax.psum_scatter(partial_term, 'split', scatter_dimension=0, tiled=True)  184 us
    all_gather x1, waiting for transfers between devices, on_device(): lax.all_gather(windowed, 'pair', axis=1, tiled=True)  166 us
    dot_general x1, matrix products, on_device(): jnp.dot(integrals, lax.all_gather(windowed, 'pair', axis=1, tiled=True),...  10.8 us
    unnamed x3, local copies, waits for them, and re-layouts  8.94 us
  transfers between devices with their start and end apart: 2, of which 2 were waited for; matrix products, arithmetic and copies ran while one was open for 0% of the time, Pallas kernels for 0%

commit v1 on v0

v1 whole, which is shorter than its diff:
```python
import jax
import jax.numpy as jnp
from jax import lax
from jax.experimental import pallas as pl
from jax.experimental.pallas import tpu as pltpu
from jax.sharding import PartitionSpec as P

MESH = pl.DeviceIdType.MESH
QS = 640
BF16, F32 = jnp.bfloat16, jnp.float32


DELTA = (0, 1, -1, 2, -2, 3, -3, 4)
PLACE = {delta: at for at, delta in enumerate(DELTA)} | {-4: 7}
Z_ORDER = (
    ((0, 1), (0, 2), (0, 3), (0, 4), (1, 1), (1, 2), (1, 3)),
    ((0, 1), (0, 2), (0, 3), (1, 1), (1, 2), (1, 3), (1, 4)),
)
Y_ORDER = tuple(
    tuple((d, j) for d in (1, 2, 3) for j in range(4)) + tuple((4, j) for j in last)
    for last in ((0, 1), (2, 3))
)
BATCHES = (((0, 5), (5, 7), (7, 8)), ((0, 8),))


def schedule():
    events = [(2.5 + 1.8 * j, "a", j) for j in (1, 2, 3)]
    for way in (0, 1):
        events += [(6.0 + 1.64 * (i + 1) + 3.0, "y", (way, i)) for i in range(14)]
        events += [(5.0 + 3.3 * (i + 1) + 2.0, "z", (way, i)) for i in range(7)]
    events.sort(key=lambda event: event[0])
    return [event[1:] for event in events]


def kernel(
    a_ref, b_ref, w_ref, out_ref, am, ab, bb, cb, rb, sb, ob,
    a_s, a_r, y_s, y_r, z_s, z_r, k_s, k_r, x_s, x_r, o_s, o_r,
):
    pair, split = lax.axis_index("pair"), lax.axis_index("split")
    zh, y, core = pair // 16, (pair // 2) % 8, pair % 2
    x, zl = split // 4, split % 4
    z = zh * 4 + zl
    exchange = (zl, zl + 1 - 2 * (zl % 2), (zl + 2) % 4, 3 - zl)

    def device(x=x, y=y, z=z, core=core):
        return (z // 4 * 16 + y * 2 + core, x * 4 + z % 4)

    def remote(src, dst, send, recv, to):
        return pltpu.make_async_remote_copy(
            src_ref=src, dst_ref=dst, send_sem=send, recv_sem=recv, device_id=to, device_id_type=MESH
        )

    def up(v, by, n):
        return (v + by + n) % n

    partners = [device(z=zh * 4 + exchange[j]) for j in (1, 2, 3)]
    partners += [device(y=up(y, d, 8)) for d in range(1, 8)]
    partners += [device(x=up(x, d, 4)) for d in (1, 2, 3)]
    partners += [device(core=1 - core), device(z=up(z, 1, 8)), device(z=up(z, -1, 8))]
    barrier = pltpu.get_barrier_semaphore()
    for partner in partners:
        pl.semaphore_signal(barrier, inc=1, device_id=partner, device_id_type=MESH)

    def k_lanes(z_lo):
        return pl.ds(pl.multiple_of(z_lo * QS, 128), QS)

    def k_rows(z):
        return pl.ds(pl.multiple_of(z * QS, 128), QS)

    my_lanes = pl.ds(pl.multiple_of(core * 128, 128), 128)

    keep = w_ref[...].astype(F32).astype(BF16)
    for xx in range(4):
        for zz in range(4):
            at = (xx * 4 + zz) * 16
            am[zz, xx * 16 : xx * 16 + 16, :] = a_ref[at : at + 16, :] * keep
    ab[0, :, k_lanes(zl)] = am[zl]
    for h in (0, 1):
        bb[h, k_rows(z), my_lanes] = b_ref[:, h * 128 : h * 128 + 128]
    pl.semaphore_wait(barrier, len(partners))

    sent = []

    def start(copy):
        copy.start()
        sent.append(copy)

    def a_copy(j):
        return remote(
            am.at[exchange[j]], ab.at[0, :, k_lanes(zl)], a_s.at[j - 1], a_r.at[j - 1],
            device(z=zh * 4 + exchange[j]),
        )

    def y_copy(way, i):
        d, j = Y_ORDER[way][i]
        sign = (-1, 1)[way]
        lanes = k_lanes(exchange[j])
        return remote(
            ab.at[PLACE[sign * (d - 1)], :, lanes], ab.at[PLACE[sign * d], :, lanes],
            y_s.at[way, i], y_r.at[way, i], device(y=up(y, -sign, 8)),
        )

    def z_copy(way, i):
        h, d = Z_ORDER[way][i]
        sign = (-1, 1)[way]
        piece = bb.at[h, k_rows(up(z, sign * (d - 1), 8)), my_lanes]
        return remote(piece, piece, z_s.at[way, i], z_r.at[way, i], device(z=up(z, -sign, 8)))

    def k_copy(h, away):
        piece = bb.at[h, k_rows(up(z, away, 8)), my_lanes]
        at = (away + 8) % 8
        return remote(piece, piece, k_s.at[h, at], k_r.at[h, at], device(core=1 - core))

    def x_copy(h, batch, d):
        lo, hi = BATCHES[h][batch]
        to = up(x, d, 4)
        at = 3 * h + batch
        return remote(
            cb.at[h, to, lo:hi], rb.at[h, d - 1, lo:hi], x_s.at[at, d - 1], x_r.at[at, d - 1], device(x=to)
        )

    def o_copy(h, place):
        return remote(
            sb.at[h, place], ob.at[h, PLACE[-DELTA[place]]], o_s.at[h, place - 1],
            o_r.at[h, PLACE[-DELTA[place]] - 1], device(y=up(y, DELTA[place], 8)),
        )

    def product(h, lo, hi):
        rows = ab[lo:hi].reshape((hi - lo) * 64, 4 * QS)
        for half in (0, 1):
            part = jnp.dot(
                rows, bb[h, half * 4 * QS : (half + 1) * 4 * QS, :], preferred_element_type=F32
            ).reshape(hi - lo, 4, 16, 256)
            for xx in range(4):
                cb[h, xx, lo:hi, :, half * 256 : half * 256 + 256] = part[:, xx]

    def total(h, batch):
        lo, hi = BATCHES[h][batch]
        for d in (1, 2, 3):
            x_copy(h, batch, d).wait_recv()
        mine = cb[h, x, lo:hi] + rb[h, 0, lo:hi] + rb[h, 1, lo:hi] + rb[h, 2, lo:hi]
        sb[h, lo:hi] = mine.astype(BF16)
        for place in range(max(lo, 1), hi):
            start(o_copy(h, place))

    def place_result(h, place, piece):
        col = up(y, DELTA[place], 8) * 512 + h * 128
        for half in (0, 1):
            for cc in (0, 1):
                to = pl.multiple_of(half * 4096 + col + cc * 256, 128)
                from_ = half * 256 + cc * 128
                out_ref[:, pl.ds(to, 128)] = piece[:, from_ : from_ + 128]

    for j in (1, 2, 3):
        start(a_copy(j))
    for way in (0, 1):
        start(y_copy(way, 0))
        start(z_copy(way, 0))
    start(k_copy(0, 0))
    start(k_copy(1, 0))

    done = set()

    def step(kind, what):
        if kind == "a":
            a_copy(what).wait_recv()
            for way in (0, 1):
                start(y_copy(way, what))
        elif kind == "y":
            way, i = what
            y_copy(way, i).wait_recv()
            d, j = Y_ORDER[way][i]
            if (d + 1, j) in Y_ORDER[way]:
                start(y_copy(way, Y_ORDER[way].index((d + 1, j))))
        else:
            way, i = what
            z_copy(way, i).wait_recv()
            h, d = Z_ORDER[way][i]
            if (h, d + 1) in Z_ORDER[way]:
                start(z_copy(way, Z_ORDER[way].index((h, d + 1))))
            if (h, d) == (0, 2):
                start(z_copy(way, Z_ORDER[way].index((1, 1))))
            start(k_copy(h, (-1, 1)[way] * d))
        done.add((kind, what))

    def wait_cores(h):
        for at in range(8):
            k_copy(h, at).wait_recv()

    h0_done = False
    sums = []
    for kind, what in schedule():
        step(kind, what)
        if not h0_done and all(("z", (way, i)) in done for way in (0, 1) for i in range(7) if Z_ORDER[way][i][0] == 0):
            wait_cores(0)
            h0_done = True
        if h0_done:
            for batch, (lo, hi) in enumerate(BATCHES[0]):
                far = {5: 2, 7: 3, 8: 4}[hi]
                ready = all(
                    ("y", (way, i)) in done for way in (0, 1) for i in range(14) if Y_ORDER[way][i][0] <= far
                )
                if ready and batch not in sums:
                    sums.append(batch)
                    product(0, lo, hi)
                    for d in (2, 1, 3):
                        start(x_copy(0, batch, d))
    wait_cores(1)
    product(1, 0, 8)
    for d in (2, 1, 3):
        start(x_copy(1, 0, d))
    for batch in range(3):
        total(0, batch)
    place_result(0, 0, sb.at[0, 0])
    for place in range(1, 8):
        o_copy(0, PLACE[-DELTA[place]]).wait_recv()
        place_result(0, place, ob.at[0, place])
    total(1, 0)
    place_result(1, 0, sb.at[1, 0])
    for place in range(1, 8):
        o_copy(1, PLACE[-DELTA[place]]).wait_recv()
        place_result(1, place, ob.at[1, place])
    for copy in sent:
        copy.wait_send()


def on_device(integrals, normal_ops, window):
    dma = pltpu.SemaphoreType.DMA
    vmem = pl.BlockSpec(memory_space=pltpu.VMEM)
    return pl.pallas_call(
        kernel,
        out_shape=jax.ShapeDtypeStruct((16, 8192), BF16),
        in_specs=[vmem] * 3,
        out_specs=vmem,
        scratch_shapes=[
            pltpu.VMEM((4, 64, QS), BF16),
            pltpu.VMEM((8, 64, 4 * QS), BF16),
            pltpu.VMEM((2, 8 * QS, 256), BF16),
            pltpu.VMEM((2, 4, 8, 16, 512), F32),
            pltpu.VMEM((2, 3, 8, 16, 512), F32),
            pltpu.VMEM((2, 8, 16, 512), BF16),
            pltpu.VMEM((2, 8, 16, 512), BF16),
            dma((3,)), dma((3,)),
            dma((2, 14)), dma((2, 14)),
            dma((2, 7)), dma((2, 7)),
            dma((2, 8)), dma((2, 8)),
            dma((4, 3)), dma((4, 3)),
            dma((2, 7)), dma((2, 7)),
        ],
        compiler_params=pltpu.CompilerParams(
            collective_id=0, has_side_effects=True, vmem_limit_bytes=48 << 20
        ),
        cost_estimate=pl.CostEstimate(flops=2 * 512 * 1024 * 2560, bytes_accessed=1 << 20, transcendentals=0),
    )(integrals, normal_ops, window.reshape(1, QS))


def solution(mesh):
    placed = (P("pair", "split"), P("split", "pair"), P("split"))
    return jax.shard_map(
        on_device, mesh=mesh, in_specs=placed, out_specs=P(("pair", "split"), None), check_vma=False
    )
```

time: 389 us -> 85 us (0.22)
  waiting for transfers between devices: 351 us -> 0 us
  Pallas kernels: 0 us -> 81.4 us
  between operations: 13.4 us -> 0.01 us
  matrix products: 10.8 us -> 0 us
  local copies, waits for them, and re-layouts: 8.94 us -> 3.34 us
  other arithmetic: 4.36 us -> 0 us
    reduce_scatter x1 -> x0, waiting for transfers between devices: 184 us -> none  [on_device(): lax.psum_scatter(partial_term, 'split', scatter_dimension=0, tiled=True)]
    all_gather x1 -> x0, waiting for transfers between devices: 166 us -> none  [on_device(): lax.all_gather(windowed, 'pair', axis=1, tiled=True)]
    pallas_call x0 -> x1, Pallas kernels: none -> 81.4 us  [on_device(): pl.pallas_call(kernel, out_shape=jax.ShapeDtypeStruct((16, 8192), BF16),...]
    dot_general x1 -> x0, matrix products: 10.8 us -> none  [on_device(): jnp.dot(integrals, lax.all_gather(windowed, 'pair', axis=1, tiled=True),...]
    unnamed x3 -> x5, local copies, waits for them, and re-layouts: 8.94 us -> 2.65 us
  transfers between devices with their start and end apart: 2 -> 0, of which waited for: 2 -> 0; matrix products, arithmetic and copies ran while one was open for 0% -> 0% of each run, Pallas kernels for 0% -> 0%
where the time goes in v1:
time: 85 us; the launch traced here: 84.7 us
  Pallas kernels  81.4 us (96%)
  local copies, waits for them, and re-layouts  3.34 us (4%)
    pallas_call x1, Pallas kernels, on_device(): pl.pallas_call(kernel, out_shape=jax.ShapeDtypeStruct((16, 8192), BF16),...  81.4 us
    unnamed x5, local copies, waits for them, and re-layouts  2.65 us

profile of v1, /device:TPU:1, one launch (start us, length us, event | category | flops | bytes accessed | tf_op | source)
XLA Modules:
  0.0 84.7 jit_solution(15956664706360254721)
XLA Ops:
  0.0 0.7 reshape.3.w_ref
  0.7 0.0 copy-start
  0.7 1.0 %copy-done = bf16[256,640]{1,0:T(8,128)(2,1)S(1)} copy-done((bf16[256,640]{1,0:T(8,128)(2,1)S(1)}, bf16[256,640]{1,0:T(8,128)(2,1)}, u32[]{:S(2)}) %copy-start) | copy-done | bytes 327704
  1.7 0.0 copy-start.1
  1.7 1.0 %copy-done.1 = bf16[640,256]{1,0:T(8,128)(2,1)S(1)} copy-done((bf16[640,256]{1,0:T(8,128)(2,1)S(1)}, bf16[640,256]{1,0:T(8,128)(2,1)}, u32[]{:S(2)}) %copy-start.1) | copy-done | bytes 327704
  2.6 81.4 %shard_map.37 = bf16[16,8192]{1,0:T(8,128)(2,1)S(1)} custom-call(bf16[256,640]{1,0:T(8,128)(2,1)S(1)} %copy-done, bf16[640,256]{1,0:T(8,128)(2,1)S(1)} %copy-done.1, s32[1,640]{1,0:T(1,128)S(1)} %reshape.3.w_ref), custom_call_target="tpu_custom_call" | custom-call | flops 2684354560 | bytes 1048576 | tf_op jit(solution)/shard_map/pallas_call | solution.py:230
  84.0 0.7 copy.5
Async XLA Ops:
  0.7 1.0 %copy-start = (bf16[256,640]{1,0:T(8,128)(2,1)S(1)}, bf16[256,640]{1,0:T(8,128)(2,1)}, u32[]{:S(2)}) copy-start(bf16[256,640]{1,0:T(8,128)(2,1)} %a_ref.1) | copy-start | bytes 983044
  1.7 1.0 %copy-start.1 = (bf16[640,256]{1,0:T(8,128)(2,1)S(1)}, bf16[640,256]{1,0:T(8,128)(2,1)}, u32[]{:S(2)}) copy-start(bf16[640,256]{1,0:T(8,128)(2,1)} %b_ref.1) | copy-start | bytes 983044

commit v2 on v1

--- a/solution.py
+++ b/solution.py
@@ -12,10 +12,10 @@
 
 DELTA = (0, 1, -1, 2, -2, 3, -3, 4)
 PLACE = {delta: at for at, delta in enumerate(DELTA)} | {-4: 7}
-Z_ORDER = (
-    ((0, 1), (0, 2), (0, 3), (0, 4), (1, 1), (1, 2), (1, 3)),
-    ((0, 1), (0, 2), (0, 3), (1, 1), (1, 2), (1, 3), (1, 4)),
+Z_ORDER = tuple(
+    tuple((h, d, k) for h in (0, 1) for d in (1, 2, 3, 4) for k in (0, 1) if d < 4 or k == way) for way in (0, 1)
 )
+KS = QS // 2
 Y_ORDER = tuple(
     tuple((d, j) for d in (1, 2, 3) for j in range(4)) + tuple((4, j) for j in last)
     for last in ((0, 1), (2, 3))
@@ -23,18 +23,51 @@
 BATCHES = (((0, 5), (5, 7), (7, 8)), ((0, 8),))
 
 
-def schedule():
-    events = [(2.5 + 1.8 * j, "a", j) for j in (1, 2, 3)]
+def schedule(latency=2.2, piece=1.64):
+    free, coming, order = {}, [], []
+
+    def send(axis, way, what, load=1.0):
+        end = max(send.now, free.get((axis, way), 0.0)) + load * piece
+        free[axis, way] = end
+        coming.append((end + latency, len(order) + len(coming), axis, way, what))
+
+    send.now = 0.0
     for way in (0, 1):
-        events += [(6.0 + 1.64 * (i + 1) + 3.0, "y", (way, i)) for i in range(14)]
-        events += [(5.0 + 3.3 * (i + 1) + 2.0, "z", (way, i)) for i in range(7)]
-    events.sort(key=lambda event: event[0])
-    return [event[1:] for event in events]
+        send("y", way, 0)
+        for j, k in ((1, 0), (2, 1), (3, None)):
+            send("z", way, ("a", j), 1.0 if j == 1 else 1.5)
+            if k is not None:
+                send("z", way, Z_ORDER[way].index((0, 1, k)))
+    while coming:
+        coming.sort()
+        send.now, _, axis, way, what = coming.pop(0)
+        if isinstance(what, tuple):
+            if way == 0:
+                order.append(what)
+                for to in (0, 1):
+                    send("y", to, what[1])
+            continue
+        order.append((axis, (way, what)))
+        for after in follow_y(way, what) if axis == "y" else follow_z(way, what):
+            send(axis, way, after)
+    return order
+
+
+def follow_y(way, i):
+    d, j = Y_ORDER[way][i]
+    return [Y_ORDER[way].index((d + 1, j))] if (d + 1, j) in Y_ORDER[way] else []
+
+
+def follow_z(way, i):
+    h, d, k = Z_ORDER[way][i]
+    after = [(h, d + 1, k)] if (h, d + 1, k) in Z_ORDER[way] else []
+    after += {(0, 1, 1): [(1, 1, 0)], (0, 2, 1): [(1, 1, 1)]}.get((h, d, k), [])
+    return [Z_ORDER[way].index(piece) for piece in after]
 
 
 def kernel(
-    a_ref, b_ref, w_ref, out_ref, am, ab, bb, cb, rb, sb, ob,
-    a_s, a_r, y_s, y_r, z_s, z_r, k_s, k_r, x_s, x_r, o_s, o_r,
+    a_ref, b_ref, w_ref, out_ref, av, wv, am, ab, bb, cb, rb, sb, ob,
+    l_s, a_s, a_r, y_s, y_r, z_s, z_r, k_s, k_r, x_s, x_r, o_s, o_r,
 ):
     pair, split = lax.axis_index("pair"), lax.axis_index("split")
     zh, y, core = pair // 16, (pair // 2) % 8, pair % 2
@@ -64,19 +97,33 @@
     def k_lanes(z_lo):
         return pl.ds(pl.multiple_of(z_lo * QS, 128), QS)
 
-    def k_rows(z):
-        return pl.ds(pl.multiple_of(z * QS, 128), QS)
+    def k_rows(z, k=None):
+        if k is None:
+            return pl.ds(pl.multiple_of(z * QS, 64), QS)
+        return pl.ds(pl.multiple_of(z * QS + k * KS, 64), KS)
 
     my_lanes = pl.ds(pl.multiple_of(core * 128, 128), 128)
 
-    keep = w_ref[...].astype(F32).astype(BF16)
+    loads = [
+        pltpu.make_async_copy(w_ref, wv, l_s.at[0]),
+        pltpu.make_async_copy(a_ref, av, l_s.at[1]),
+    ] + [
+        pltpu.make_async_copy(b_ref.at[:, pl.ds(h * 128, 128)], bb.at[h, k_rows(z), my_lanes], l_s.at[2 + h])
+        for h in (0, 1)
+    ]
+    for load in loads:
+        load.start()
+    cb[1] = jnp.zeros(cb.shape[1:], F32)
+    for load in loads[:2]:
+        load.wait()
+    keep = wv[...].astype(F32).astype(BF16).reshape(1, QS)
     for xx in range(4):
         for zz in range(4):
             at = (xx * 4 + zz) * 16
-            am[zz, xx * 16 : xx * 16 + 16, :] = a_ref[at : at + 16, :] * keep
+            am[zz, xx * 16 : xx * 16 + 16, :] = av[at : at + 16, :] * keep
     ab[0, :, k_lanes(zl)] = am[zl]
-    for h in (0, 1):
-        bb[h, k_rows(z), my_lanes] = b_ref[:, h * 128 : h * 128 + 128]
+    for load in loads[2:]:
+        load.wait()
     pl.semaphore_wait(barrier, len(partners))
 
     sent = []
@@ -101,14 +148,14 @@
         )
 
     def z_copy(way, i):
-        h, d = Z_ORDER[way][i]
+        h, d, k = Z_ORDER[way][i]
         sign = (-1, 1)[way]
-        piece = bb.at[h, k_rows(up(z, sign * (d - 1), 8)), my_lanes]
+        piece = bb.at[h, k_rows(up(z, sign * (d - 1), 8), k), my_lanes]
         return remote(piece, piece, z_s.at[way, i], z_r.at[way, i], device(z=up(z, -sign, 8)))
 
-    def k_copy(h, away):
-        piece = bb.at[h, k_rows(up(z, away, 8)), my_lanes]
-        at = (away + 8) % 8
+    def k_copy(h, away, k):
+        piece = bb.at[h, k_rows(up(z, away, 8), k), my_lanes]
+        at = (away + 8) % 8 * 2 + k
         return remote(piece, piece, k_s.at[h, at], k_r.at[h, at], device(core=1 - core))
 
     def x_copy(h, batch, d):
@@ -151,13 +198,16 @@
                 from_ = half * 256 + cc * 128
                 out_ref[:, pl.ds(to, 128)] = piece[:, from_ : from_ + 128]
 
-    for j in (1, 2, 3):
-        start(a_copy(j))
     for way in (0, 1):
         start(y_copy(way, 0))
-        start(z_copy(way, 0))
-    start(k_copy(0, 0))
-    start(k_copy(1, 0))
+    for j, k in ((1, 0), (2, 1), (3, None)):
+        start(a_copy(j))
+        if k is not None:
+            for way in (0, 1):
+                start(z_copy(way, Z_ORDER[way].index((0, 1, k))))
+    for h in (0, 1):
+        for k in (0, 1):
+            start(k_copy(h, 0, k))
 
     done = set()
 
@@ -169,30 +219,37 @@
         elif kind == "y":
             way, i = what
             y_copy(way, i).wait_recv()
-            d, j = Y_ORDER[way][i]
-            if (d + 1, j) in Y_ORDER[way]:
-                start(y_copy(way, Y_ORDER[way].index((d + 1, j))))
+            for after in follow_y(way, i):
+                start(y_copy(way, after))
         else:
             way, i = what
             z_copy(way, i).wait_recv()
-            h, d = Z_ORDER[way][i]
-            if (h, d + 1) in Z_ORDER[way]:
-                start(z_copy(way, Z_ORDER[way].index((h, d + 1))))
-            if (h, d) == (0, 2):
-                start(z_copy(way, Z_ORDER[way].index((1, 1))))
-            start(k_copy(h, (-1, 1)[way] * d))
+            for after in follow_z(way, i):
+                start(z_copy(way, after))
+            h, d, k = Z_ORDER[way][i]
+            start(k_copy(h, (-1, 1)[way] * d, k))
         done.add((kind, what))
 
-    def wait_cores(h):
-        for at in range(8):
-            k_copy(h, at).wait_recv()
+    def wait_core(h, at):
+        for k in (0, 1):
+            k_copy(h, at, k).wait_recv()
+
+    def add_product(at):
+        owner = up(z, at, 8)
+        lanes = pl.ds(pl.multiple_of(owner // 4 * 256, 128), 256)
+        part = jnp.dot(
+            ab[:, :, k_lanes(owner % 4)].reshape(512, QS), bb[1, k_rows(owner), :], preferred_element_type=F32
+        ).reshape(8, 4, 16, 256)
+        for xx in range(4):
+            cb[1, xx, :, :, lanes] += part[:, xx]
 
     h0_done = False
     sums = []
     for kind, what in schedule():
         step(kind, what)
-        if not h0_done and all(("z", (way, i)) in done for way in (0, 1) for i in range(7) if Z_ORDER[way][i][0] == 0):
-            wait_cores(0)
+        if not h0_done and all(("z", (way, i)) in done for way in (0, 1) for i in range(14) if Z_ORDER[way][i][0] == 0):
+            for at in range(8):
+                wait_core(0, at)
             h0_done = True
         if h0_done:
             for batch, (lo, hi) in enumerate(BATCHES[0]):
@@ -205,8 +262,9 @@
                     product(0, lo, hi)
                     for d in (2, 1, 3):
                         start(x_copy(0, batch, d))
-    wait_cores(1)
-    product(1, 0, 8)
+    for at in (0, 1, 7, 2, 6, 3, 5, 4):
+        wait_core(1, at)
+        add_product(at)
     for d in (2, 1, 3):
         start(x_copy(1, 0, d))
     for batch in range(3):
@@ -230,9 +288,11 @@
     return pl.pallas_call(
         kernel,
         out_shape=jax.ShapeDtypeStruct((16, 8192), BF16),
-        in_specs=[vmem] * 3,
+        in_specs=[pl.BlockSpec(memory_space=pl.ANY)] * 3,
         out_specs=vmem,
         scratch_shapes=[
+            pltpu.VMEM((256, QS), BF16),
+            pltpu.VMEM((QS,), jnp.int32),
             pltpu.VMEM((4, 64, QS), BF16),
             pltpu.VMEM((8, 64, 4 * QS), BF16),
             pltpu.VMEM((2, 8 * QS, 256), BF16),
@@ -240,18 +300,19 @@
             pltpu.VMEM((2, 3, 8, 16, 512), F32),
             pltpu.VMEM((2, 8, 16, 512), BF16),
             pltpu.VMEM((2, 8, 16, 512), BF16),
+            dma((4,)),
             dma((3,)), dma((3,)),
             dma((2, 14)), dma((2, 14)),
-            dma((2, 7)), dma((2, 7)),
-            dma((2, 8)), dma((2, 8)),
+            dma((2, 14)), dma((2, 14)),
+            dma((2, 16)), dma((2, 16)),
             dma((4, 3)), dma((4, 3)),
             dma((2, 7)), dma((2, 7)),
         ],
         compiler_params=pltpu.CompilerParams(
-            collective_id=0, has_side_effects=True, vmem_limit_bytes=48 << 20
+            collective_id=0, has_side_effects=True, vmem_limit_bytes=54848 << 10
         ),
         cost_estimate=pl.CostEstimate(flops=2 * 512 * 1024 * 2560, bytes_accessed=1 << 20, transcendentals=0),
-    )(integrals, normal_ops, window.reshape(1, QS))
+    )(integrals, normal_ops, window)
 
 
 def solution(mesh):

time: 85 us -> 77.5 us (0.912); the launches traced: 84.7 us -> 76.3 us
  Pallas kernels: 81.4 us -> 74.9 us
  local copies, waits for them, and re-layouts: 3.34 us -> 1.39 us
    pallas_call x1, Pallas kernels: 81.4 us -> 74.9 us  [on_device(): pl.pallas_call(kernel, out_shape=jax.ShapeDtypeStruct((16, 8192), BF16),...]
    unnamed x5 -> x3, local copies, waits for them, and re-layouts: 2.65 us -> 1.39 us
where the time goes in v2:
time: 77.5 us; the launch traced here: 76.3 us
  Pallas kernels  74.9 us (97%)
  local copies, waits for them, and re-layouts  1.39 us (2%)
    pallas_call x1, Pallas kernels, on_device(): pl.pallas_call(kernel, out_shape=jax.ShapeDtypeStruct((16, 8192), BF16),...  74.9 us

profile of v2, /device:TPU:1, one launch (start us, length us, event | category | flops | bytes accessed | tf_op | source)
XLA Modules:
  0.0 76.3 jit_solution(321128281038266293)
XLA Ops:
  0.0 0.0 copy-start
  0.0 0.7 copy-done
  0.7 74.9 %shard_map.37 = bf16[16,8192]{1,0:T(8,128)(2,1)S(1)} custom-call(bf16[256,640]{1,0:T(8,128)(2,1)} %a_ref.1, bf16[640,256]{1,0:T(8,128)(2,1)} %b_ref.1, s32[640]{0:T(1024)S(1)} %copy-done), custom_call_target="tpu_custom_call" | custom-call | flops 2684354560 | bytes 1048576 | tf_op jit(solution)/shard_map/pallas_call | solution.py:288
  75.6 0.7 copy.5
Async XLA Ops:
  0.0 0.7 copy-start

commit v3 on v2

--- a/solution.py
+++ b/solution.py
@@ -13,14 +13,16 @@
 DELTA = (0, 1, -1, 2, -2, 3, -3, 4)
 PLACE = {delta: at for at, delta in enumerate(DELTA)} | {-4: 7}
 Z_ORDER = tuple(
-    tuple((h, d, k) for h in (0, 1) for d in (1, 2, 3, 4) for k in (0, 1) if d < 4 or k == way) for way in (0, 1)
+    tuple((h, d, k) for h in (0, 1) for d in (1, 2, 3, 4) for k in range(4) if d < 4 or k // 2 == way) for way in (0, 1)
 )
-KS = QS // 2
+KS = QS // 4
 Y_ORDER = tuple(
     tuple((d, j) for d in (1, 2, 3) for j in range(4)) + tuple((4, j) for j in last)
     for last in ((0, 1), (2, 3))
 )
-BATCHES = (((0, 5), (5, 7), (7, 8)), ((0, 8),))
+BATCHES = (((0, 5), (5, 7), (7, 8)), ((4, 8), (0, 4)))
+MOST = 32767.0
+FIRST = ((1, (0, 1)), (2, (2, 3)), (3, ()))
 
 
 def schedule(latency=2.2, piece=1.64):
@@ -34,10 +36,10 @@
     send.now = 0.0
     for way in (0, 1):
         send("y", way, 0)
-        for j, k in ((1, 0), (2, 1), (3, None)):
+        for j, runs in FIRST:
             send("z", way, ("a", j), 1.0 if j == 1 else 1.5)
-            if k is not None:
-                send("z", way, Z_ORDER[way].index((0, 1, k)))
+            for k in runs:
+                send("z", way, Z_ORDER[way].index((0, 1, k)), 0.5)
     while coming:
         coming.sort()
         send.now, _, axis, way, what = coming.pop(0)
@@ -49,7 +51,7 @@
             continue
         order.append((axis, (way, what)))
         for after in follow_y(way, what) if axis == "y" else follow_z(way, what):
-            send(axis, way, after)
+            send(axis, way, after, 1.0 if axis == "y" else 0.5)
     return order
 
 
@@ -61,12 +63,13 @@
 def follow_z(way, i):
     h, d, k = Z_ORDER[way][i]
     after = [(h, d + 1, k)] if (h, d + 1, k) in Z_ORDER[way] else []
-    after += {(0, 1, 1): [(1, 1, 0)], (0, 2, 1): [(1, 1, 1)]}.get((h, d, k), [])
+    if (h, d) == (0, 3):
+        after.append((1, 1, k))
     return [Z_ORDER[way].index(piece) for piece in after]
 
 
 def kernel(
-    a_ref, b_ref, w_ref, out_ref, av, wv, am, ab, bb, cb, rb, sb, ob,
+    a_ref, b_ref, w_ref, out_ref, av, wv, am, ab, bb, cb, qb, qs, rb, rs, sb, ob,
     l_s, a_s, a_r, y_s, y_r, z_s, z_r, k_s, k_r, x_s, x_r, o_s, o_r,
 ):
     pair, split = lax.axis_index("pair"), lax.axis_index("split")
@@ -100,7 +103,7 @@
     def k_rows(z, k=None):
         if k is None:
             return pl.ds(pl.multiple_of(z * QS, 64), QS)
-        return pl.ds(pl.multiple_of(z * QS + k * KS, 64), KS)
+        return pl.ds(pl.multiple_of(z * QS + k * KS, 32), KS)
 
     my_lanes = pl.ds(pl.multiple_of(core * 128, 128), 128)
 
@@ -114,6 +117,7 @@
     for load in loads:
         load.start()
     cb[1] = jnp.zeros(cb.shape[1:], F32)
+    qs[...] = jnp.zeros(qs.shape, F32)
     for load in loads[:2]:
         load.wait()
     keep = wv[...].astype(F32).astype(BF16).reshape(1, QS)
@@ -154,17 +158,35 @@
         return remote(piece, piece, z_s.at[way, i], z_r.at[way, i], device(z=up(z, -sign, 8)))
 
     def k_copy(h, away, k):
-        piece = bb.at[h, k_rows(up(z, away, 8), k), my_lanes]
+        rows = pl.ds(pl.multiple_of(up(z, away, 8) * QS + k * 2 * KS, 64), 2 * KS)
+        piece = bb.at[h, rows, my_lanes]
         at = (away + 8) % 8 * 2 + k
         return remote(piece, piece, k_s.at[h, at], k_r.at[h, at], device(core=1 - core))
 
-    def x_copy(h, batch, d):
+    def x_copies(h, batch, d):
         lo, hi = BATCHES[h][batch]
-        to = up(x, d, 4)
         at = 3 * h + batch
-        return remote(
-            cb.at[h, to, lo:hi], rb.at[h, d - 1, lo:hi], x_s.at[at, d - 1], x_r.at[at, d - 1], device(x=to)
-        )
+        return (
+            remote(
+                qb.at[h, d - 1, lo:hi], rb.at[h, d - 1, lo:hi], x_s.at[at, d - 1, 0], x_r.at[at, d - 1, 0],
+                device(x=up(x, d, 4)),
+            ),
+            remote(
+                qs.at[at, d - 1], rs.at[at, d - 1], x_s.at[at, d - 1, 1], x_r.at[at, d - 1, 1],
+                device(x=up(x, d, 4)),
+            ),
+        )
+
+    def send_sums(h, batch):
+        lo, hi = BATCHES[h][batch]
+        at = 3 * h + batch
+        for d in (2, 1, 3):
+            part = cb[h, up(x, d, 4), lo:hi]
+            top = jnp.maximum(jnp.max(jnp.abs(part), axis=1, keepdims=True), 1e-30)
+            qb[h, d - 1, lo:hi] = jnp.round(part * (MOST / top)).astype(jnp.int32).astype(jnp.int16)
+            qs[at, d - 1, 0 : hi - lo, :] = (top * (1.0 / MOST)).reshape(hi - lo, 512)
+            for copy in x_copies(h, batch, d):
+                start(copy)
 
     def o_copy(h, place):
         return remote(
@@ -183,9 +205,13 @@
 
     def total(h, batch):
         lo, hi = BATCHES[h][batch]
+        at = 3 * h + batch
+        mine = cb[h, x, lo:hi]
         for d in (1, 2, 3):
-            x_copy(h, batch, d).wait_recv()
-        mine = cb[h, x, lo:hi] + rb[h, 0, lo:hi] + rb[h, 1, lo:hi] + rb[h, 2, lo:hi]
+            for copy in x_copies(h, batch, d):
+                copy.wait_recv()
+            step = rs[at, d - 1, 0 : hi - lo, :].reshape(hi - lo, 1, 512)
+            mine += rb[h, d - 1, lo:hi].astype(jnp.int32).astype(F32) * step
         sb[h, lo:hi] = mine.astype(BF16)
         for place in range(max(lo, 1), hi):
             start(o_copy(h, place))
@@ -200,9 +226,9 @@
 
     for way in (0, 1):
         start(y_copy(way, 0))
-    for j, k in ((1, 0), (2, 1), (3, None)):
+    for j, runs in FIRST:
         start(a_copy(j))
-        if k is not None:
+        for k in runs:
             for way in (0, 1):
                 start(z_copy(way, Z_ORDER[way].index((0, 1, k))))
     for h in (0, 1):
@@ -227,7 +253,8 @@
             for after in follow_z(way, i):
                 start(z_copy(way, after))
             h, d, k = Z_ORDER[way][i]
-            start(k_copy(h, (-1, 1)[way] * d, k))
+            if k % 2:
+                start(k_copy(h, (-1, 1)[way] * d, k // 2))
         done.add((kind, what))
 
     def wait_core(h, at):
@@ -247,7 +274,7 @@
     sums = []
     for kind, what in schedule():
         step(kind, what)
-        if not h0_done and all(("z", (way, i)) in done for way in (0, 1) for i in range(14) if Z_ORDER[way][i][0] == 0):
+        if not h0_done and all(("z", (way, i)) in done for way in (0, 1) for i in range(28) if Z_ORDER[way][i][0] == 0):
             for at in range(8):
                 wait_core(0, at)
             h0_done = True
@@ -260,13 +287,12 @@
                 if ready and batch not in sums:
                     sums.append(batch)
                     product(0, lo, hi)
-                    for d in (2, 1, 3):
-                        start(x_copy(0, batch, d))
+                    send_sums(0, batch)
     for at in (0, 1, 7, 2, 6, 3, 5, 4):
         wait_core(1, at)
         add_product(at)
-    for d in (2, 1, 3):
-        start(x_copy(1, 0, d))
+    for batch in (0, 1):
+        send_sums(1, batch)
     for batch in range(3):
         total(0, batch)
     place_result(0, 0, sb.at[0, 0])
@@ -274,6 +300,7 @@
         o_copy(0, PLACE[-DELTA[place]]).wait_recv()
         place_result(0, place, ob.at[0, place])
     total(1, 0)
+    total(1, 1)
     place_result(1, 0, sb.at[1, 0])
     for place in range(1, 8):
         o_copy(1, PLACE[-DELTA[place]]).wait_recv()
@@ -297,15 +324,18 @@
             pltpu.VMEM((8, 64, 4 * QS), BF16),
             pltpu.VMEM((2, 8 * QS, 256), BF16),
             pltpu.VMEM((2, 4, 8, 16, 512), F32),
-            pltpu.VMEM((2, 3, 8, 16, 512), F32),
+            pltpu.VMEM((2, 3, 8, 16, 512), jnp.int16),
+            pltpu.VMEM((5, 3, 8, 512), F32),
+            pltpu.VMEM((2, 3, 8, 16, 512), jnp.int16),
+            pltpu.VMEM((5, 3, 8, 512), F32),
             pltpu.VMEM((2, 8, 16, 512), BF16),
             pltpu.VMEM((2, 8, 16, 512), BF16),
             dma((4,)),
             dma((3,)), dma((3,)),
             dma((2, 14)), dma((2, 14)),
-            dma((2, 14)), dma((2, 14)),
+            dma((2, 28)), dma((2, 28)),
             dma((2, 16)), dma((2, 16)),
-            dma((4, 3)), dma((4, 3)),
+            dma((5, 3, 2)), dma((5, 3, 2)),
             dma((2, 7)), dma((2, 7)),
         ],
         compiler_params=pltpu.CompilerParams(

time: 77.5 us -> 74 us (0.955); the launches traced: 76.3 us -> 73.8 us
  Pallas kernels: 74.9 us -> 72.4 us
    pallas_call x1, Pallas kernels: 74.9 us -> 72.4 us  [on_device(): pl.pallas_call(kernel, out_shape=jax.ShapeDtypeStruct((16, 8192), BF16),...]
where the time goes in v3:
time: 74 us; the launch traced here: 73.8 us
  Pallas kernels  72.4 us (98%)
  local copies, waits for them, and re-layouts  1.39 us (2%)
    pallas_call x1, Pallas kernels, on_device(): pl.pallas_call(kernel, out_shape=jax.ShapeDtypeStruct((16, 8192), BF16),...  72.4 us

profile of v3, /device:TPU:1, one launch (start us, length us, event | category | flops | bytes accessed | tf_op | source)
XLA Modules:
  0.0 73.8 jit_solution(16000552614272458207)
XLA Ops:
  0.0 0.0 copy-start
  0.0 0.7 copy-done
  0.7 72.4 %shard_map.37 = bf16[16,8192]{1,0:T(8,128)(2,1)S(1)} custom-call(bf16[256,640]{1,0:T(8,128)(2,1)} %a_ref.1, bf16[640,256]{1,0:T(8,128)(2,1)} %b_ref.1, s32[640]{0:T(1024)S(1)} %copy-done), custom_call_target="tpu_custom_call" | custom-call | flops 2684354560 | bytes 1048576 | tf_op jit(solution)/shard_map/pallas_call | solution.py:315
  73.1 0.7 copy.5
Async XLA Ops:
  0.0 0.7 copy-start

commit v4 on v3

--- a/solution.py
+++ b/solution.py
@@ -20,12 +20,13 @@
     tuple((d, j) for d in (1, 2, 3) for j in range(4)) + tuple((4, j) for j in last)
     for last in ((0, 1), (2, 3))
 )
-BATCHES = (((0, 5), (5, 7), (7, 8)), ((4, 8), (0, 4)))
+BATCHES = (((0, 4), (4, 8)), ((4, 8), (0, 4)))
 MOST = 32767.0
-FIRST = ((1, (0, 1)), (2, (2, 3)), (3, ()))
-
-
-def schedule(latency=2.2, piece=1.64):
+NEAR_FIRST = (0, 1, 7, 2, 6, 3, 5, 4)
+FIRST = (("a", 1), ("z", (0, 1)), ("a", 2), ("z", (2, 3)), ("a", 3))
+
+
+def schedule(latency=3.2, piece=1.64):
     free, coming, order = {}, [], []
 
     def send(axis, way, what, load=1.0):
@@ -36,10 +37,12 @@
     send.now = 0.0
     for way in (0, 1):
         send("y", way, 0)
-        for j, runs in FIRST:
-            send("z", way, ("a", j), 1.0 if j == 1 else 1.5)
-            for k in runs:
-                send("z", way, Z_ORDER[way].index((0, 1, k)), 0.5)
+        for kind, what in FIRST:
+            if kind == "a":
+                send("z", way, ("a", what), 1.0 if what == 1 else 1.5)
+            else:
+                for k in what:
+                    send("z", way, Z_ORDER[way].index((0, 1, k)), 0.5)
     while coming:
         coming.sort()
         send.now, _, axis, way, what = coming.pop(0)
@@ -63,7 +66,7 @@
 def follow_z(way, i):
     h, d, k = Z_ORDER[way][i]
     after = [(h, d + 1, k)] if (h, d + 1, k) in Z_ORDER[way] else []
-    if (h, d) == (0, 3):
+    if (h, d) == (0, 1):
         after.append((1, 1, k))
     return [Z_ORDER[way].index(piece) for piece in after]
 
@@ -117,17 +120,6 @@
     for load in loads:
         load.start()
     cb[1] = jnp.zeros(cb.shape[1:], F32)
-    qs[...] = jnp.zeros(qs.shape, F32)
-    for load in loads[:2]:
-        load.wait()
-    keep = wv[...].astype(F32).astype(BF16).reshape(1, QS)
-    for xx in range(4):
-        for zz in range(4):
-            at = (xx * 4 + zz) * 16
-            am[zz, xx * 16 : xx * 16 + 16, :] = av[at : at + 16, :] * keep
-    ab[0, :, k_lanes(zl)] = am[zl]
-    for load in loads[2:]:
-        load.wait()
     pl.semaphore_wait(barrier, len(partners))
 
     sent = []
@@ -135,6 +127,10 @@
     def start(copy):
         copy.start()
         sent.append(copy)
+
+    def drain(n):
+        for _ in range(n):
+            sent.pop(0).wait_send()
 
     def a_copy(j):
         return remote(
@@ -155,17 +151,19 @@
         h, d, k = Z_ORDER[way][i]
         sign = (-1, 1)[way]
         piece = bb.at[h, k_rows(up(z, sign * (d - 1), 8), k), my_lanes]
-        return remote(piece, piece, z_s.at[way, i], z_r.at[way, i], device(z=up(z, -sign, 8)))
+        own = b_ref.at[pl.ds(k * KS, KS), pl.ds(h * 128, 128)]
+        return remote(own if d == 1 else piece, piece, z_s.at[way, i], z_r.at[way, i], device(z=up(z, -sign, 8)))
 
     def k_copy(h, away, k):
         rows = pl.ds(pl.multiple_of(up(z, away, 8) * QS + k * 2 * KS, 64), 2 * KS)
         piece = bb.at[h, rows, my_lanes]
         at = (away + 8) % 8 * 2 + k
-        return remote(piece, piece, k_s.at[h, at], k_r.at[h, at], device(core=1 - core))
+        own = b_ref.at[pl.ds(k * 2 * KS, 2 * KS), pl.ds(h * 128, 128)]
+        return remote(piece if away else own, piece, k_s.at[h, at], k_r.at[h, at], device(core=1 - core))
 
     def x_copies(h, batch, d):
         lo, hi = BATCHES[h][batch]
-        at = 3 * h + batch
+        at = 2 * h + batch
         return (
             remote(
                 qb.at[h, d - 1, lo:hi], rb.at[h, d - 1, lo:hi], x_s.at[at, d - 1, 0], x_r.at[at, d - 1, 0],
@@ -179,12 +177,14 @@
 
     def send_sums(h, batch):
         lo, hi = BATCHES[h][batch]
-        at = 3 * h + batch
+        at = 2 * h + batch
         for d in (2, 1, 3):
             part = cb[h, up(x, d, 4), lo:hi]
             top = jnp.maximum(jnp.max(jnp.abs(part), axis=1, keepdims=True), 1e-30)
             qb[h, d - 1, lo:hi] = jnp.round(part * (MOST / top)).astype(jnp.int32).astype(jnp.int16)
-            qs[at, d - 1, 0 : hi - lo, :] = (top * (1.0 / MOST)).reshape(hi - lo, 512)
+            step = (top * (1.0 / MOST)).reshape(4, 512)
+            qs[at, d - 1, 0:4, :] = step[:, :256]
+            qs[at, d - 1, 4:8, :] = step[:, 256:]
             for copy in x_copies(h, batch, d):
                 start(copy)
 
@@ -205,12 +205,12 @@
 
     def total(h, batch):
         lo, hi = BATCHES[h][batch]
-        at = 3 * h + batch
+        at = 2 * h + batch
         mine = cb[h, x, lo:hi]
         for d in (1, 2, 3):
             for copy in x_copies(h, batch, d):
                 copy.wait_recv()
-            step = rs[at, d - 1, 0 : hi - lo, :].reshape(hi - lo, 1, 512)
+            step = jnp.concatenate([rs[at, d - 1, 0:4, :], rs[at, d - 1, 4:8, :]], axis=1).reshape(4, 1, 512)
             mine += rb[h, d - 1, lo:hi].astype(jnp.int32).astype(F32) * step
         sb[h, lo:hi] = mine.astype(BF16)
         for place in range(max(lo, 1), hi):
@@ -224,16 +224,30 @@
                 from_ = half * 256 + cc * 128
                 out_ref[:, pl.ds(to, 128)] = piece[:, from_ : from_ + 128]
 
-    for way in (0, 1):
-        start(y_copy(way, 0))
-    for j, runs in FIRST:
-        start(a_copy(j))
-        for k in runs:
+    for kind, what in FIRST:
+        if kind == "z":
+            for k in what:
+                for way in (0, 1):
+                    start(z_copy(way, Z_ORDER[way].index((0, 1, k))))
+            continue
+        if what == 1:
+            for load in loads[:2]:
+                load.wait()
+            keep = wv[...].astype(F32).astype(BF16).reshape(1, QS)
+            for zz in range(4):
+                for xx in range(4):
+                    at = (xx * 4 + zz) * 16
+                    am[zz, xx * 16 : xx * 16 + 16, :] = av[at : at + 16, :] * keep
+            ab[0, :, k_lanes(zl)] = am[zl]
+        start(a_copy(what))
+        if what == 1:
             for way in (0, 1):
-                start(z_copy(way, Z_ORDER[way].index((0, 1, k))))
+                start(y_copy(way, 0))
     for h in (0, 1):
         for k in (0, 1):
             start(k_copy(h, 0, k))
+    for load in loads[2:]:
+        load.wait()
 
     done = set()
 
@@ -270,8 +284,12 @@
         for xx in range(4):
             cb[1, xx, :, :, lanes] += part[:, xx]
 
+    def ready(far):
+        return all(("y", (way, i)) in done for way in (0, 1) for i in range(14) if Y_ORDER[way][i][0] <= far)
+
     h0_done = False
     sums = []
+    behind = list(NEAR_FIRST)
     for kind, what in schedule():
         step(kind, what)
         if not h0_done and all(("z", (way, i)) in done for way in (0, 1) for i in range(28) if Z_ORDER[way][i][0] == 0):
@@ -280,21 +298,26 @@
             h0_done = True
         if h0_done:
             for batch, (lo, hi) in enumerate(BATCHES[0]):
-                far = {5: 2, 7: 3, 8: 4}[hi]
-                ready = all(
-                    ("y", (way, i)) in done for way in (0, 1) for i in range(14) if Y_ORDER[way][i][0] <= far
-                )
-                if ready and batch not in sums:
+                far = {4: 2, 8: 4}[hi]
+                if ready(far) and batch not in sums:
                     sums.append(batch)
                     product(0, lo, hi)
                     send_sums(0, batch)
-    for at in (0, 1, 7, 2, 6, 3, 5, 4):
+        if len(sums) == 2:
+            arrived = {Z_ORDER[way][i][1] for way in (0, 1) for i in range(28) if ("z", (way, i)) in done and i + 2 < 28 and ("z", (way, i + 2)) in done and Z_ORDER[way][i][0] == 1 and Z_ORDER[way][i][2] == 3}
+            if behind and (behind[0] == 0 or min(behind[0], 8 - behind[0]) in arrived):
+                at = behind.pop(0)
+                wait_core(1, at)
+                add_product(at)
+    for at in behind:
         wait_core(1, at)
         add_product(at)
+    gathered = len(sent)
     for batch in (0, 1):
         send_sums(1, batch)
-    for batch in range(3):
+    for batch in (0, 1):
         total(0, batch)
+    drain(gathered)
     place_result(0, 0, sb.at[0, 0])
     for place in range(1, 8):
         o_copy(0, PLACE[-DELTA[place]]).wait_recv()
@@ -305,8 +328,7 @@
     for place in range(1, 8):
         o_copy(1, PLACE[-DELTA[place]]).wait_recv()
         place_result(1, place, ob.at[1, place])
-    for copy in sent:
-        copy.wait_send()
+    drain(len(sent))
 
 
 def on_device(integrals, normal_ops, window):
@@ -325,9 +347,9 @@
             pltpu.VMEM((2, 8 * QS, 256), BF16),
             pltpu.VMEM((2, 4, 8, 16, 512), F32),
             pltpu.VMEM((2, 3, 8, 16, 512), jnp.int16),
-            pltpu.VMEM((5, 3, 8, 512), F32),
+            pltpu.VMEM((4, 3, 8, 256), F32),
             pltpu.VMEM((2, 3, 8, 16, 512), jnp.int16),
-            pltpu.VMEM((5, 3, 8, 512), F32),
+            pltpu.VMEM((4, 3, 8, 256), F32),
             pltpu.VMEM((2, 8, 16, 512), BF16),
             pltpu.VMEM((2, 8, 16, 512), BF16),
             dma((4,)),
@@ -335,7 +357,7 @@
             dma((2, 14)), dma((2, 14)),
             dma((2, 28)), dma((2, 28)),
             dma((2, 16)), dma((2, 16)),
-            dma((5, 3, 2)), dma((5, 3, 2)),
+            dma((4, 3, 2)), dma((4, 3, 2)),
             dma((2, 7)), dma((2, 7)),
         ],
         compiler_params=pltpu.CompilerParams(

time: 74 us -> 68.7 us (0.928)
  Pallas kernels: 72.4 us -> 67.2 us
    pallas_call x1, Pallas kernels: 72.4 us -> 67.2 us  [on_device(): pl.pallas_call(kernel, out_shape=jax.ShapeDtypeStruct((16, 8192), BF16),...]
where the time goes in v4:
time: 68.7 us; the launch traced here: 68.6 us
  Pallas kernels  67.2 us (98%)
  local copies, waits for them, and re-layouts  1.39 us (2%)
    pallas_call x1, Pallas kernels, on_device(): pl.pallas_call(kernel, out_shape=jax.ShapeDtypeStruct((16, 8192), BF16),...  67.2 us
    unnamed x3, local copies, waits for them, and re-layouts  1.39 us

profile of v4, /device:TPU:1, one launch (start us, length us, event | category | flops | bytes accessed | tf_op | source)
XLA Modules:
  0.0 68.6 jit_solution(15685674418188230749)
XLA Ops:
  0.0 0.0 copy-start
  0.0 0.7 copy-done
  0.7 67.2 %shard_map.37 = bf16[16,8192]{1,0:T(8,128)(2,1)S(1)} custom-call(bf16[256,640]{1,0:T(8,128)(2,1)} %a_ref.1, bf16[640,256]{1,0:T(8,128)(2,1)} %b_ref.1, s32[640]{0:T(1024)S(1)} %copy-done), custom_call_target="tpu_custom_call" | custom-call | flops 2684354560 | bytes 1048576 | tf_op jit(solution)/shard_map/pallas_call | solution.py:337
  67.9 0.7 %copy.5 = bf16[16,8192]{1,0:T(8,128)(2,1)} copy(bf16[16,8192]{1,0:T(8,128)(2,1)S(1)} %shard_map.37) | data formatting | bytes 524288
Async XLA Ops:
  0.0 0.7 %copy-start = (s32[640]{0:T(1024)S(1)}, s32[640]{0:T(1024)}, u32[]{:S(2)}) copy-start(s32[640]{0:T(1024)} %w_ref.1) | copy-start | bytes 7684

commit v5 on v4

v5 whole, which is shorter than its diff:
```python
import jax
import jax.numpy as jnp
from jax import lax
from jax.experimental import pallas as pl
from jax.experimental.pallas import tpu as pltpu
from jax.sharding import PartitionSpec as P

MESH = pl.DeviceIdType.MESH
QS = 640
BF16, F32 = jnp.bfloat16, jnp.float32


DELTA = (0, 1, -1, 2, -2, 3, -3, 4)
PLACE = {delta: at for at, delta in enumerate(DELTA)} | {-4: 7}
Z_ORDER = tuple(
    tuple((h, d, k) for h in (0, 1) for d in (1, 2, 3, 4) for k in range(2) if d < 4 or k == way) for way in (0, 1)
)
KS = QS // 2
Y_ORDER = tuple(
    tuple((d, j) for d in (1, 2, 3) for j in range(4)) + tuple((4, j) for j in last)
    for last in ((0, 1), (2, 3))
)
MOST = 32600.0
NEAR_FIRST = (0, 1, 7, 2, 6, 3, 5, 4)
FIRST = (("a", 1), ("z", (0,)), ("a", 2), ("z", (1,)), ("a", 3))


def schedule(latency=3.2, piece=1.64, core=3.0):
    free, coming, order = {}, [], []

    def send(axis, way, what, load=1.0):
        end = max(send.now, free.get((axis, way), 0.0)) + load * piece
        free[axis, way] = end
        coming.append((end + latency, len(order) + len(coming), axis, way, what))

    send.now = 0.0
    for way in (0, 1):
        send("y", way, 0)
        for kind, what in FIRST:
            if kind == "a":
                send("z", way, ("a", what), 1.0 if what == 1 else 1.5)
            else:
                for k in what:
                    send("z", way, Z_ORDER[way].index((0, 1, k)))
    while coming:
        coming.sort()
        send.now, _, axis, way, what = coming.pop(0)
        if isinstance(what, tuple):
            if way == 0:
                order.append((send.now, *what))
                for to in (0, 1):
                    send("y", to, what[1])
            continue
        order.append((send.now, axis, (way, what)))
        for after in follow_y(way, what) if axis == "y" else follow_z(way, what):
            send(axis, way, after)
    rows = {far: max(t for t, axis, (way, i) in heard(order, "y") if Y_ORDER[way][i][0] <= far) for far in (2, 4)}
    columns = {(h, at): 0.0 for h in (0, 1) for at in range(8)}
    for t, _, (way, i) in heard(order, "z"):
        h, d, _ = Z_ORDER[way][i]
        at = (-d if way == 0 else d) % 8
        columns[h, at] = max(t, columns[h, at]) + 0.0
    first = max(t for (h, _), t in columns.items() if h == 0) + core
    order.append((max(rows[2], first), "p", 0))
    order.append((max(rows[4], first), "p", 1))
    after = max(rows[4], first)
    for at in NEAR_FIRST:
        after = max(after + 0.3, columns[1, at] + core)
        order.append((after, "q", at))
    order.sort(key=lambda event: event[0])
    return [event[1:] for event in order]


def heard(order, axis):
    return [event for event in order if event[1] == axis]


def follow_y(way, i):
    d, j = Y_ORDER[way][i]
    return [Y_ORDER[way].index((d + 1, j))] if (d + 1, j) in Y_ORDER[way] else []


def follow_z(way, i):
    h, d, k = Z_ORDER[way][i]
    after = [(h, d + 1, k)] if (h, d + 1, k) in Z_ORDER[way] else []
    if (h, d) == (0, 2):
        after.append((1, 1, k))
    return [Z_ORDER[way].index(piece) for piece in after]


def kernel(
    a_ref, b_ref, w_ref, out_ref, w0, w1, w2, w3, wf, ab, bb, cb, qb, qs, rb, rs, sb, ob,
    l_s, w_s, w_r, a_s, a_r, y_s, y_r, z_s, z_r, k_s, k_r, x_s, x_r, o_s, o_r,
):
    pair, split = lax.axis_index("pair"), lax.axis_index("split")
    zh, y, core = pair // 16, (pair // 2) % 8, pair % 2
    x, zl = split // 4, split % 4
    z = zh * 4 + zl
    exchange = (zl, zl + 1 - 2 * (zl % 2), (zl + 2) % 4, 3 - zl)

    def device(x=x, y=y, z=z, core=core):
        return (z // 4 * 16 + y * 2 + core, x * 4 + z % 4)

    def remote(src, dst, send, recv, to):
        return pltpu.make_async_remote_copy(
            src_ref=src, dst_ref=dst, send_sem=send, recv_sem=recv, device_id=to, device_id_type=MESH
        )

    def up(v, by, n):
        return (v + by + n) % n

    partners = [device(z=zh * 4 + exchange[j]) for j in (1, 2, 3)]
    partners += [device(y=up(y, d, 8)) for d in range(1, 8)]
    partners += [device(x=up(x, d, 4)) for d in (1, 2, 3)]
    partners += [device(core=1 - core), device(z=up(z, 1, 8)), device(z=up(z, -1, 8))]
    barrier = pltpu.get_barrier_semaphore()
    for partner in partners:
        pl.semaphore_signal(barrier, inc=1, device_id=partner, device_id_type=MESH)

    def k_lanes(z_lo):
        return pl.ds(pl.multiple_of(z_lo * QS, 128), QS)

    def k_rows(z, k=None):
        if k is None:
            return pl.ds(pl.multiple_of(z * QS, 64), QS)
        return pl.ds(pl.multiple_of(z * QS + k * KS, 32), KS)

    my_lanes = pl.ds(pl.multiple_of(core * 128, 128), 128)

    ws = (w0, w1, w2, w3)
    loads = [
        pltpu.make_async_copy(w_ref, w0, l_s.at[0]),
        pltpu.make_async_copy(a_ref.at[:, zl], ab.at[0, :, :, k_lanes(zl)], l_s.at[1]),
    ] + [
        pltpu.make_async_copy(b_ref.at[:, pl.ds(h * 128, 128)], bb.at[h, k_rows(z), my_lanes], l_s.at[2 + h])
        for h in (0, 1)
    ]
    for load in loads:
        load.start()
    cb[1] = jnp.zeros(cb.shape[1:], F32)
    pl.semaphore_wait(barrier, len(partners))

    sent = []

    def start(copy):
        copy.start()
        sent.append(copy)

    def drain(n):
        for _ in range(n):
            sent.pop(0).wait_send()

    def a_copy(j):
        return remote(
            a_ref.at[:, exchange[j]], ab.at[0, :, :, k_lanes(zl)], a_s.at[j - 1], a_r.at[j - 1],
            device(z=zh * 4 + exchange[j]),
        )

    def w_copy(j):
        return remote(w_ref, ws[j], w_s.at[j - 1], w_r.at[j - 1], device(z=zh * 4 + exchange[j]))

    def y_copy(way, i):
        d, j = Y_ORDER[way][i]
        sign = (-1, 1)[way]
        lanes = k_lanes(exchange[j])
        own = a_ref.at[:, zl]
        return remote(
            own if i == 0 else ab.at[PLACE[sign * (d - 1)], :, :, lanes], ab.at[PLACE[sign * d], :, :, lanes],
            y_s.at[way, i], y_r.at[way, i], device(y=up(y, -sign, 8)),
        )

    def z_copy(way, i):
        h, d, k = Z_ORDER[way][i]
        sign = (-1, 1)[way]
        piece = bb.at[h, k_rows(up(z, sign * (d - 1), 8), k), my_lanes]
        own = b_ref.at[pl.ds(k * KS, KS), pl.ds(h * 128, 128)]
        return remote(own if d == 1 else piece, piece, z_s.at[way, i], z_r.at[way, i], device(z=up(z, -sign, 8)))

    def k_copy(h, away, k):
        rows = pl.ds(pl.multiple_of(up(z, away, 8) * QS + k * KS, 64), KS)
        piece = bb.at[h, rows, my_lanes]
        at = (away + 8) % 8 * 2 + k
        own = b_ref.at[pl.ds(k * KS, KS), pl.ds(h * 128, 128)]
        return remote(piece if away else own, piece, k_s.at[h, at], k_r.at[h, at], device(core=1 - core))

    def x_copies(batch, d):
        to = device(x=up(x, d, 4))
        return tuple(
            remote(src.at[batch, d - 1], dst.at[batch, d - 1], x_s.at[batch, d - 1, at], x_r.at[batch, d - 1, at], to)
            for at, (src, dst) in enumerate(((qb, rb), (qs, rs)))
        )

    def units(batch):
        if batch < 2:
            lo, hi = batch * 4, batch * 4 + 4
            return ((0, 4, 0, 0, lo, hi), (4, 8, 0, 1, lo, hi))
        return ((0, 8, 1, (zh, 1 - zh)[batch - 2], 0, 8),)

    def send_sums(batch):
        for d in (2, 1, 3):
            steps = []
            for at, end, h, half, lo, hi in units(batch):
                part = cb[h, half, up(x, d, 4), lo:hi]
                top = jnp.maximum(jnp.max(jnp.abs(part), axis=1, keepdims=True), 1e-30)
                step = (top * (1.0 / MOST)).astype(BF16).astype(F32)
                qb[batch, d - 1, at:end] = jnp.round(part / step).astype(jnp.int32).astype(jnp.int16)
                steps.append(step.reshape(end - at, 256))
            steps = jnp.concatenate(steps, axis=0)
            qs[batch, d - 1] = jnp.concatenate([steps[:, :128], steps[:, 128:]], axis=0).astype(BF16)
            for copy in x_copies(batch, d):
                start(copy)

    def o_copy(batch, place):
        there = PLACE[-DELTA[place]]
        if batch < 2:
            src, dst = sb.at[0, place], ob.at[0, there]
        else:
            half = (zh, 1 - zh)[batch - 2]
            src, dst = sb.at[1, place, half], ob.at[1, there, half]
        at = max(batch - 1, 0)
        return remote(
            src, dst, o_s.at[at, place - 1], o_r.at[at, there - 1], device(y=up(y, DELTA[place], 8))
        )

    def total(batch):
        for d in (1, 2, 3):
            for copy in x_copies(batch, d):
                copy.wait_recv()
        for at, end, h, half, lo, hi in units(batch):
            mine = cb[h, half, x, lo:hi]
            for d in (1, 2, 3):
                steps = rs[batch, d - 1].astype(F32)
                step = jnp.concatenate([steps[at:end], steps[8 + at : 8 + end]], axis=1).reshape(end - at, 1, 256)
                mine += rb[batch, d - 1, at:end].astype(jnp.int32).astype(F32) * step
            sb[h, lo:hi, half] = mine.astype(BF16)
        for place in range(max(lo, 1), hi):
            start(o_copy(batch, place))

    def rows_of(block, w):
        return (block * w.reshape(1, 1, 1, w.shape[-1])).reshape(-1, w.shape[-1])

    def arrive_local():
        for load in loads:
            load.wait()
        for j in (1, 2, 3):
            w_copy(j).wait_recv()
        for j in range(4):
            wf[exchange[j]] = ws[j][...].astype(F32).astype(BF16).reshape(1, QS)

    def product(lo, hi):
        rows = rows_of(ab[lo:hi], jnp.concatenate([wf[at] for at in range(4)], axis=1))
        for half in (0, 1):
            part = jnp.dot(
                rows, bb[0, half * 4 * QS : (half + 1) * 4 * QS, :], preferred_element_type=F32
            ).reshape(hi - lo, 4, 16, 256)
            for xx in range(4):
                cb[0, half, xx, lo:hi] = part[:, xx]

    def add_product(at):
        owner = up(z, at, 8)
        part = jnp.dot(
            rows_of(ab[:, :, :, k_lanes(owner % 4)], wf[owner % 4]), bb[1, k_rows(owner), :],
            preferred_element_type=F32,
        ).reshape(8, 4, 16, 256)
        for xx in range(4):
            cb[1, owner // 4, xx] += part[:, xx]

    def wait_core(h, at):
        for k in (0, 1):
            k_copy(h, at, k).wait_recv()

    def place_result(h, place, half, piece):
        for cc in (0, 1):
            to = pl.multiple_of(half * 4096 + up(y, DELTA[place], 8) * 512 + cc * 256 + h * 128, 128)
            out_ref[:, pl.ds(to, 128)] = piece[:, cc * 128 : cc * 128 + 128]

    def place_all(batch):
        h = min(batch - 1, 1)
        for half in (0, 1) if h == 0 else ((zh, 1 - zh)[batch - 2],):
            place_result(h, 0, half, sb[h, 0, half])
        for place in range(1, 8):
            o_copy(batch, PLACE[-DELTA[place]]).wait_recv()
            for half in (0, 1) if h == 0 else ((zh, 1 - zh)[batch - 2],):
                place_result(h, place, half, ob[h, place, half])

    for kind, what in FIRST:
        if kind == "z":
            for k in what:
                for way in (0, 1):
                    start(z_copy(way, Z_ORDER[way].index((0, 1, k))))
            continue
        start(a_copy(what))
        if what == 1:
            for way in (0, 1):
                start(y_copy(way, 0))
    for h in (0, 1):
        for k in (0, 1):
            start(k_copy(h, 0, k))
    for j in (1, 2, 3):
        start(w_copy(j))

    def step(kind, what):
        if kind == "a":
            a_copy(what).wait_recv()
            for way in (0, 1):
                start(y_copy(way, what))
        elif kind == "y":
            way, i = what
            y_copy(way, i).wait_recv()
            for after in follow_y(way, i):
                start(y_copy(way, after))
        else:
            way, i = what
            z_copy(way, i).wait_recv()
            for after in follow_z(way, i):
                start(z_copy(way, after))
            h, d, k = Z_ORDER[way][i]
            start(k_copy(h, (-1, 1)[way] * d, k))

    for count, (kind, what) in enumerate(schedule()):
        if kind in "ayz":
            step(kind, what)
            if count > 30:
                drain(2)
        elif kind == "p":
            if what == 0:
                arrive_local()
                for at in range(8):
                    wait_core(0, at)
            product(what * 4, what * 4 + 4)
            send_sums(what)
        else:
            if what == 4:
                send_sums(2)
                total(0)
            wait_core(1, what)
            add_product(what)
    gathered = len(sent)
    send_sums(3)
    total(1)
    total(2)
    drain(gathered)
    place_all(1)
    total(3)
    drain(len(sent) - 7)
    place_all(2)
    place_all(3)
    drain(len(sent))


def on_device(integrals, normal_ops, window):
    dma = pltpu.SemaphoreType.DMA
    vmem = pl.BlockSpec(memory_space=pltpu.VMEM)
    return pl.pallas_call(
        kernel,
        out_shape=jax.ShapeDtypeStruct((16, 8192), BF16),
        in_specs=[pl.BlockSpec(memory_space=pl.ANY)] * 3,
        out_specs=vmem,
        scratch_shapes=[
            pltpu.VMEM((QS,), jnp.int32),
            pltpu.VMEM((QS,), jnp.int32),
            pltpu.VMEM((QS,), jnp.int32),
            pltpu.VMEM((QS,), jnp.int32),
            pltpu.VMEM((4, 1, QS), BF16),
            pltpu.VMEM((8, 4, 16, 4 * QS), BF16),
            pltpu.VMEM((2, 8 * QS, 256), BF16),
            pltpu.VMEM((2, 2, 4, 8, 16, 256), F32),
            pltpu.VMEM((4, 3, 8, 16, 256), jnp.int16),
            pltpu.VMEM((4, 3, 16, 128), BF16),
            pltpu.VMEM((4, 3, 8, 16, 256), jnp.int16),
            pltpu.VMEM((4, 3, 16, 128), BF16),
            pltpu.VMEM((2, 8, 2, 16, 256), BF16),
            pltpu.VMEM((2, 8, 2, 16, 256), BF16),
            dma((4,)),
            dma((3,)), dma((3,)),
            dma((3,)), dma((3,)),
            dma((2, 14)), dma((2, 14)),
            dma((2, 14)), dma((2, 14)),
            dma((2, 16)), dma((2, 16)),
            dma((4, 3, 2)), dma((4, 3, 2)),
            dma((3, 7)), dma((3, 7)),
        ],
        compiler_params=pltpu.CompilerParams(
            collective_id=0, has_side_effects=True, vmem_limit_bytes=54848 << 10
        ),
        cost_estimate=pl.CostEstimate(flops=2 * 512 * 1024 * 2560, bytes_accessed=1 << 20, transcendentals=0),
    )(integrals.reshape(4, 4, 16, QS), normal_ops, window)


def solution(mesh):
    placed = (P("pair", "split"), P("split", "pair"), P("split"))
    return jax.shard_map(
        on_device, mesh=mesh, in_specs=placed, out_specs=P(("pair", "split"), None), check_vma=False
    )
```

time: 68.7 us -> 67.5 us (0.983)
  Pallas kernels: 67.2 us -> 66 us
    pallas_call x1, Pallas kernels: 67.2 us -> 66 us  [on_device(): pl.pallas_call(kernel, out_shape=jax.ShapeDtypeStruct((16, 8192), BF16),...]
where the time goes in v5:
time: 67.5 us; the launch traced here: 67.4 us
  Pallas kernels  66 us (98%)
  local copies, waits for them, and re-layouts  1.39 us (2%)
    pallas_call x1, Pallas kernels, on_device(): pl.pallas_call(kernel, out_shape=jax.ShapeDtypeStruct((16, 8192), BF16),...  66 us
    unnamed x3, local copies, waits for them, and re-layouts  1.39 us

profile of v5, /device:TPU:1, one launch (start us, length us, event | category | flops | bytes accessed | tf_op | source)
XLA Modules:
  0.0 67.4 jit_solution(5906903101240486634)
XLA Ops:
  0.0 0.0 copy-start
  0.0 0.7 %copy-done = s32[640]{0:T(1024)S(1)} copy-done((s32[640]{0:T(1024)S(1)}, s32[640]{0:T(1024)}, u32[]{:S(2)}) %copy-start) | copy-done | bytes 2584
  0.7 66.0 %shard_map.37 = bf16[16,8192]{1,0:T(8,128)(2,1)S(1)} custom-call(bf16[4,4,16,640]{3,2,1,0:T(8,128)(2,1)} %bitcast.1, bf16[640,256]{1,0:T(8,128)(2,1)} %b_ref.1, s32[640]{0:T(1024)S(1)} %copy-done), custom_call_target="tpu_custom_call" | custom-call | flops 2684354560 | bytes 1048576 | tf_op jit(solution)/shard_map/pallas_call | solution.py:354
  66.7 0.7 %copy.5 = bf16[16,8192]{1,0:T(8,128)(2,1)} copy(bf16[16,8192]{1,0:T(8,128)(2,1)S(1)} %shard_map.37) | data formatting | bytes 524288
Async XLA Ops:
  0.0 0.7 %copy-start = (s32[640]{0:T(1024)S(1)}, s32[640]{0:T(1024)}, u32[]{:S(2)}) copy-start(s32[640]{0:T(1024)} %w_ref.1) | copy-start | bytes 7684

commit v6 on v5

--- a/solution.py
+++ b/solution.py
@@ -21,58 +21,18 @@
     for last in ((0, 1), (2, 3))
 )
 MOST = 32600.0
-NEAR_FIRST = (0, 1, 7, 2, 6, 3, 5, 4)
-FIRST = (("a", 1), ("z", (0,)), ("a", 2), ("z", (1,)), ("a", 3))
-
-
-def schedule(latency=3.2, piece=1.64, core=3.0):
-    free, coming, order = {}, [], []
-
-    def send(axis, way, what, load=1.0):
-        end = max(send.now, free.get((axis, way), 0.0)) + load * piece
-        free[axis, way] = end
-        coming.append((end + latency, len(order) + len(coming), axis, way, what))
-
-    send.now = 0.0
-    for way in (0, 1):
-        send("y", way, 0)
-        for kind, what in FIRST:
-            if kind == "a":
-                send("z", way, ("a", what), 1.0 if what == 1 else 1.5)
-            else:
-                for k in what:
-                    send("z", way, Z_ORDER[way].index((0, 1, k)))
-    while coming:
-        coming.sort()
-        send.now, _, axis, way, what = coming.pop(0)
-        if isinstance(what, tuple):
-            if way == 0:
-                order.append((send.now, *what))
-                for to in (0, 1):
-                    send("y", to, what[1])
-            continue
-        order.append((send.now, axis, (way, what)))
-        for after in follow_y(way, what) if axis == "y" else follow_z(way, what):
-            send(axis, way, after)
-    rows = {far: max(t for t, axis, (way, i) in heard(order, "y") if Y_ORDER[way][i][0] <= far) for far in (2, 4)}
-    columns = {(h, at): 0.0 for h in (0, 1) for at in range(8)}
-    for t, _, (way, i) in heard(order, "z"):
-        h, d, _ = Z_ORDER[way][i]
-        at = (-d if way == 0 else d) % 8
-        columns[h, at] = max(t, columns[h, at]) + 0.0
-    first = max(t for (h, _), t in columns.items() if h == 0) + core
-    order.append((max(rows[2], first), "p", 0))
-    order.append((max(rows[4], first), "p", 1))
-    after = max(rows[4], first)
-    for at in NEAR_FIRST:
-        after = max(after + 0.3, columns[1, at] + core)
-        order.append((after, "q", at))
-    order.sort(key=lambda event: event[0])
-    return [event[1:] for event in order]
-
-
-def heard(order, axis):
-    return [event for event in order if event[1] == axis]
+ORDER = (
+    ("A", 2), ("A", 1), ("i", 0, 0), ("i", 0, 1), ("y", 1, 0), ("y", 0, 0), ("A", 3), ("z", 1, 0), ("a", 1),
+    ("z", 0, 0), ("a", 2), ("i", 1, 0), ("y", 1, 1), ("z", 1, 1), ("z", 0, 1), ("y", 0, 1), ("y", 1, 4),
+    ("a", 3), ("i", 1, 1), ("y", 1, 2), ("y", 0, 4), ("z", 0, 2), ("y", 0, 2), ("z", 1, 2), ("y", 1, 5),
+    ("z", 0, 3), ("z", 1, 3), ("y", 0, 3), ("z", 0, 7), ("y", 0, 8), ("z", 1, 7), ("z", 1, 4), ("z", 1, 8),
+    ("y", 0, 6), ("y", 1, 3), ("z", 1, 5), ("y", 1, 6), ("z", 0, 8), ("z", 1, 9), ("z", 0, 4), ("y", 1, 8),
+    ("y", 0, 5), ("z", 0, 5), ("y", 1, 7), ("z", 0, 9), ("y", 0, 7), ("y", 0, 9), ("z", 1, 10), ("y", 1, 10),
+    ("z", 1, 6), ("z", 0, 10), ("y", 0, 10), ("y", 1, 11), ("y", 1, 9), ("z", 0, 6), ("p", 0), ("y", 0, 12),
+    ("z", 1, 12), ("z", 0, 11), ("z", 1, 11), ("y", 1, 12), ("y", 0, 13), ("z", 0, 12), ("y", 1, 13),
+    ("y", 0, 11), ("q", 7), ("q", 6), ("p", 1), ("q", 0), ("q", 3), ("q", 2), ("q", 5), ("z", 1, 13),
+    ("z", 0, 13), ("q", 1), ("q", 4),
+)
 
 
 def follow_y(way, i):
@@ -83,8 +43,6 @@
 def follow_z(way, i):
     h, d, k = Z_ORDER[way][i]
     after = [(h, d + 1, k)] if (h, d + 1, k) in Z_ORDER[way] else []
-    if (h, d) == (0, 2):
-        after.append((1, 1, k))
     return [Z_ORDER[way].index(piece) for piece in after]
 
 
@@ -135,9 +93,6 @@
         pltpu.make_async_copy(b_ref.at[:, pl.ds(h * 128, 128)], bb.at[h, k_rows(z), my_lanes], l_s.at[2 + h])
         for h in (0, 1)
     ]
-    for load in loads:
-        load.start()
-    cb[1] = jnp.zeros(cb.shape[1:], F32)
     pl.semaphore_wait(barrier, len(partners))
 
     sent = []
@@ -185,16 +140,21 @@
 
     def x_copies(batch, d):
         to = device(x=up(x, d, 4))
+        n = units(batch)[-1][1]
         return tuple(
-            remote(src.at[batch, d - 1], dst.at[batch, d - 1], x_s.at[batch, d - 1, at], x_r.at[batch, d - 1, at], to)
-            for at, (src, dst) in enumerate(((qb, rb), (qs, rs)))
+            remote(src, dst, x_s.at[batch, d - 1, at], x_r.at[batch, d - 1, at], to)
+            for at, (src, dst) in enumerate((
+                (qb.at[batch, d - 1, 0:n], rb.at[batch, d - 1, 0:n]), (qs.at[batch, d - 1], rs.at[batch, d - 1])
+            ))
         )
 
     def units(batch):
         if batch < 2:
             lo, hi = batch * 4, batch * 4 + 4
             return ((0, 4, 0, 0, lo, hi), (4, 8, 0, 1, lo, hi))
-        return ((0, 8, 1, (zh, 1 - zh)[batch - 2], 0, 8),)
+        if batch == 2:
+            return ((0, 8, 1, zh, 0, 8),)
+        return ((0, 4, 1, 1 - zh, (4, 0)[batch - 3], (8, 4)[batch - 3]),)
 
     def send_sums(batch):
         for d in (2, 1, 3):
@@ -205,6 +165,8 @@
                 step = (top * (1.0 / MOST)).astype(BF16).astype(F32)
                 qb[batch, d - 1, at:end] = jnp.round(part / step).astype(jnp.int32).astype(jnp.int16)
                 steps.append(step.reshape(end - at, 256))
+            if end == 4:
+                steps.append(jnp.zeros((4, 256), F32))
             steps = jnp.concatenate(steps, axis=0)
             qs[batch, d - 1] = jnp.concatenate([steps[:, :128], steps[:, 128:]], axis=0).astype(BF16)
             for copy in x_copies(batch, d):
@@ -215,9 +177,9 @@
         if batch < 2:
             src, dst = sb.at[0, place], ob.at[0, there]
         else:
-            half = (zh, 1 - zh)[batch - 2]
+            half = (zh, 1 - zh, 1 - zh)[batch - 2]
             src, dst = sb.at[1, place, half], ob.at[1, there, half]
-        at = max(batch - 1, 0)
+        at = min(max(batch - 1, 0), 2)
         return remote(
             src, dst, o_s.at[at, place - 1], o_r.at[at, there - 1], device(y=up(y, DELTA[place], 8))
         )
@@ -240,6 +202,7 @@
         return (block * w.reshape(1, 1, 1, w.shape[-1])).reshape(-1, w.shape[-1])
 
     def arrive_local():
+        cb[1] = jnp.zeros(cb.shape[1:], F32)
         for load in loads:
             load.wait()
         for j in (1, 2, 3):
@@ -283,27 +246,11 @@
             for half in (0, 1) if h == 0 else ((zh, 1 - zh)[batch - 2],):
                 place_result(h, place, half, ob[h, place, half])
 
-    for kind, what in FIRST:
-        if kind == "z":
-            for k in what:
-                for way in (0, 1):
-                    start(z_copy(way, Z_ORDER[way].index((0, 1, k))))
-            continue
-        start(a_copy(what))
-        if what == 1:
-            for way in (0, 1):
-                start(y_copy(way, 0))
-    for h in (0, 1):
-        for k in (0, 1):
-            start(k_copy(h, 0, k))
-    for j in (1, 2, 3):
-        start(w_copy(j))
-
     def step(kind, what):
         if kind == "a":
-            a_copy(what).wait_recv()
+            a_copy(what[0]).wait_recv()
             for way in (0, 1):
-                start(y_copy(way, what))
+                start(y_copy(way, what[0]))
         elif kind == "y":
             way, i = what
             y_copy(way, i).wait_recv()
@@ -317,31 +264,48 @@
             h, d, k = Z_ORDER[way][i]
             start(k_copy(h, (-1, 1)[way] * d, k))
 
-    for count, (kind, what) in enumerate(schedule()):
-        if kind in "ayz":
+    for load in loads:
+        load.start()
+    for count, (kind, *what) in enumerate(ORDER):
+        if kind == "A":
+            start(a_copy(what[0]))
+            if what[0] == 1:
+                for way in (0, 1):
+                    start(y_copy(way, 0))
+        elif kind == "i":
+            h, k = what
+            for way in (0, 1):
+                start(z_copy(way, Z_ORDER[way].index((h, 1, k))))
+            start(k_copy(h, 0, k))
+            if (h, k) == (0, 0):
+                for j in (1, 2, 3):
+                    start(w_copy(j))
+        elif kind in "ayz":
             step(kind, what)
-            if count > 30:
+            if count > 40:
                 drain(2)
         elif kind == "p":
-            if what == 0:
+            if what[0] == 0:
                 arrive_local()
                 for at in range(8):
                     wait_core(0, at)
-            product(what * 4, what * 4 + 4)
-            send_sums(what)
+            product(what[0] * 4, what[0] * 4 + 4)
+            send_sums(what[0])
         else:
-            if what == 4:
+            if what[0] == 4:
                 send_sums(2)
                 total(0)
-            wait_core(1, what)
-            add_product(what)
+            wait_core(1, what[0])
+            add_product(what[0])
     gathered = len(sent)
     send_sums(3)
+    send_sums(4)
     total(1)
     total(2)
     drain(gathered)
     place_all(1)
     total(3)
+    total(4)
     drain(len(sent) - 7)
     place_all(2)
     place_all(3)
@@ -365,10 +329,10 @@
             pltpu.VMEM((8, 4, 16, 4 * QS), BF16),
             pltpu.VMEM((2, 8 * QS, 256), BF16),
             pltpu.VMEM((2, 2, 4, 8, 16, 256), F32),
-            pltpu.VMEM((4, 3, 8, 16, 256), jnp.int16),
-            pltpu.VMEM((4, 3, 16, 128), BF16),
-            pltpu.VMEM((4, 3, 8, 16, 256), jnp.int16),
-            pltpu.VMEM((4, 3, 16, 128), BF16),
+            pltpu.VMEM((5, 3, 8, 16, 256), jnp.int16),
+            pltpu.VMEM((5, 3, 16, 128), BF16),
+            pltpu.VMEM((5, 3, 8, 16, 256), jnp.int16),
+            pltpu.VMEM((5, 3, 16, 128), BF16),
             pltpu.VMEM((2, 8, 2, 16, 256), BF16),
             pltpu.VMEM((2, 8, 2, 16, 256), BF16),
             dma((4,)),
@@ -377,14 +341,14 @@
             dma((2, 14)), dma((2, 14)),
             dma((2, 14)), dma((2, 14)),
             dma((2, 16)), dma((2, 16)),
-            dma((4, 3, 2)), dma((4, 3, 2)),
+            dma((5, 3, 2)), dma((5, 3, 2)),
             dma((3, 7)), dma((3, 7)),
         ],
         compiler_params=pltpu.CompilerParams(
             collective_id=0, has_side_effects=True, vmem_limit_bytes=54848 << 10
         ),
         cost_estimate=pl.CostEstimate(flops=2 * 512 * 1024 * 2560, bytes_accessed=1 << 20, transcendentals=0),
-    )(integrals.reshape(4, 4, 16, QS), normal_ops, window)
+    )(integrals.reshape(4, 4, 16, QS), normal_ops, pltpu.with_memory_space_constraint(window, pltpu.HBM))
 
 
 def solution(mesh):

time: 67.5 us -> 66.2 us (0.981)
  Pallas kernels: 66 us -> 64.7 us
  local copies, waits for them, and re-layouts: 1.39 us -> 0.71 us
    pallas_call x1, Pallas kernels: 66 us -> 64.7 us  [on_device(): pl.pallas_call(kernel, out_shape=jax.ShapeDtypeStruct((16, 8192), BF16),...]
    unnamed x3 -> x1, local copies, waits for them, and re-layouts: 1.39 us -> 0.71 us
where the time goes in v6:
time: 66.2 us; the launch traced here: 65.4 us
  Pallas kernels  64.7 us (98%)
  local copies, waits for them, and re-layouts  0.71 us (1%)
    pallas_call x1, Pallas kernels, on_device(): pl.pallas_call(kernel, out_shape=jax.ShapeDtypeStruct((16, 8192), BF16),...  64.7 us

profile of v6, /device:TPU:1, one launch (start us, length us, event | category | flops | bytes accessed | tf_op | source)
XLA Modules:
  0.0 65.4 jit_solution(13696110560237595389)
XLA Ops:
  0.0 64.7 %shard_map.37 = bf16[16,8192]{1,0:T(8,128)(2,1)S(1)} custom-call(bf16[4,4,16,640]{3,2,1,0:T(8,128)(2,1)} %bitcast.1, bf16[640,256]{1,0:T(8,128)(2,1)} %b_ref.1, s32[640]{0:T(1024)} %w_ref.1), custom_call_target="tpu_custom_call" | custom-call | flops 2684354560 | bytes 1048576 | tf_op jit(solution)/shard_map/pallas_call | solution.py:318
  64.7 0.7 %copy.5 = bf16[16,8192]{1,0:T(8,128)(2,1)} copy(bf16[16,8192]{1,0:T(8,128)(2,1)S(1)} %shard_map.37) | data formatting | bytes 524288

commit v7 on v6

--- a/solution.py
+++ b/solution.py
@@ -22,16 +22,16 @@
 )
 MOST = 32600.0
 ORDER = (
-    ("A", 2), ("A", 1), ("i", 0, 0), ("i", 0, 1), ("y", 1, 0), ("y", 0, 0), ("A", 3), ("z", 1, 0), ("a", 1),
-    ("z", 0, 0), ("a", 2), ("i", 1, 0), ("y", 1, 1), ("z", 1, 1), ("z", 0, 1), ("y", 0, 1), ("y", 1, 4),
-    ("a", 3), ("i", 1, 1), ("y", 1, 2), ("y", 0, 4), ("z", 0, 2), ("y", 0, 2), ("z", 1, 2), ("y", 1, 5),
-    ("z", 0, 3), ("z", 1, 3), ("y", 0, 3), ("z", 0, 7), ("y", 0, 8), ("z", 1, 7), ("z", 1, 4), ("z", 1, 8),
-    ("y", 0, 6), ("y", 1, 3), ("z", 1, 5), ("y", 1, 6), ("z", 0, 8), ("z", 1, 9), ("z", 0, 4), ("y", 1, 8),
-    ("y", 0, 5), ("z", 0, 5), ("y", 1, 7), ("z", 0, 9), ("y", 0, 7), ("y", 0, 9), ("z", 1, 10), ("y", 1, 10),
-    ("z", 1, 6), ("z", 0, 10), ("y", 0, 10), ("y", 1, 11), ("y", 1, 9), ("z", 0, 6), ("p", 0), ("y", 0, 12),
-    ("z", 1, 12), ("z", 0, 11), ("z", 1, 11), ("y", 1, 12), ("y", 0, 13), ("z", 0, 12), ("y", 1, 13),
-    ("y", 0, 11), ("q", 7), ("q", 6), ("p", 1), ("q", 0), ("q", 3), ("q", 2), ("q", 5), ("z", 1, 13),
-    ("z", 0, 13), ("q", 1), ("q", 4),
+    ("A", 3), ("A", 1), ("i", 0, 0), ("y", 1, 0), ("i", 0, 1), ("y", 0, 0), ("a", 3), ("A", 2), ("a", 1),
+    ("z", 0, 0), ("z", 1, 1), ("i", 1, 1), ("y", 0, 4), ("i", 1, 0), ("y", 1, 4), ("z", 1, 0), ("z", 0, 1),
+    ("a", 2), ("y", 0, 3), ("z", 0, 2), ("y", 1, 3), ("z", 0, 8), ("z", 1, 3), ("y", 0, 1), ("y", 1, 2),
+    ("y", 1, 1), ("y", 0, 2), ("z", 0, 7), ("z", 1, 8), ("y", 1, 7), ("z", 1, 2), ("y", 1, 6), ("y", 0, 8),
+    ("y", 0, 5), ("z", 0, 3), ("z", 1, 5), ("z", 1, 7), ("z", 0, 4), ("y", 1, 5), ("z", 0, 9), ("y", 0, 12),
+    ("y", 0, 7), ("z", 0, 10), ("z", 1, 4), ("z", 0, 5), ("z", 1, 10), ("y", 1, 10), ("y", 0, 6), ("z", 1, 6),
+    ("z", 1, 9), ("y", 1, 8), ("y", 1, 9), ("z", 0, 6), ("y", 1, 11), ("y", 0, 9), ("z", 0, 11), ("p", 0),
+    ("y", 0, 11), ("y", 0, 10), ("z", 1, 11), ("y", 0, 13), ("y", 1, 13), ("z", 1, 12), ("y", 1, 12),
+    ("z", 0, 12), ("p", 1), ("q", 2), ("q", 6), ("q", 0), ("q", 5), ("q", 3), ("q", 1), ("z", 0, 13), ("q", 7),
+    ("z", 1, 13), ("q", 4),
 )
 
 

time: 66.2 us -> 66.7 us (level)
  the two profiles are of different devices: /device:TPU:1 before, /device:TPU:8 now
where the time goes in v7:
time: 66.7 us; the launch traced here: 66.6 us
  Pallas kernels  65.9 us (99%)
  local copies, waits for them, and re-layouts  0.71 us (1%)
    pallas_call x1, Pallas kernels, on_device(): pl.pallas_call(kernel, out_shape=jax.ShapeDtypeStruct((16, 8192), BF16),...  65.9 us

profile of v7, /device:TPU:8, one launch (start us, length us, event | category | flops | bytes accessed | tf_op | source)
XLA Modules:
  0.0 66.6 jit_solution(12256345306311001370)
XLA Ops:
  0.0 65.9 %shard_map.37 = bf16[16,8192]{1,0:T(8,128)(2,1)S(1)} custom-call(bf16[4,4,16,640]{3,2,1,0:T(8,128)(2,1)} %bitcast.1, bf16[640,256]{1,0:T(8,128)(2,1)} %b_ref.1, s32[640]{0:T(1024)} %w_ref.1), custom_call_target="tpu_custom_call" | custom-call | flops 2684354560 | bytes 1048576 | tf_op jit(solution)/shard_map/pallas_call | solution.py:318
  65.9 0.7 %copy.5 = bf16[16,8192]{1,0:T(8,128)(2,1)} copy(bf16[16,8192]{1,0:T(8,128)(2,1)S(1)} %shard_map.37) | data formatting | bytes 524288
